TPU v7x, 256 devices: a whole 4x4x8 slice. The times are simulated.
256 devices in a mesh: expert: 64 (over z, y, core), tensor: 4 (over x).
Axes of the slice: x: 4, y: 4, z: 8, core: 2. Of those that a mesh axis runs over, the one named last changes fastest.
Arguments:
- attn_heads: bfloat16 [32768, 2048], P('expert', 'tensor'), may hold values from -6 to 6
- o_weight: bfloat16 [2048, 2048], P('tensor'), may hold values from -0.125 to 0.125
- resid: bfloat16 [32768, 2048], P(('expert', 'tensor')), may hold values from -6 to 6
- norm_gain: float32 [2048], replicated, may hold values from 0.1 to 1.9
- expert_ids: int32 [32768, 4], P(('expert', 'tensor')), may hold values from 0 to 63, all different within a row; in each aligned block of 128 rows (0 to 127, 128 to 255, ...) at most 11 rows name the same one
- combine_weights: float32 [32768, 4], P(('expert', 'tensor')), may hold values from 0.05 to 0.35
- w_gate_up: bfloat16 [64, 2, 2048, 1408], P('expert', None, None, 'tensor'), may hold values from -0.125 to 0.125
- w_down: bfloat16 [64, 1408, 2048], P('expert', 'tensor'), may hold values from -0.15625 to 0.15625
Outputs:
- layer_out: bfloat16 [32768, 2048], P(('expert', 'tensor'))
Inputs may be any that keep to these rules, and one draw needn't show every extreme that they name: `expert_ids`: each row names 4 different experts. In the rows of one device (128 aligned rows) no expert is named more than 11 times, and in some device's rows one expert is named exactly 11 times.
All inputs are finite; a program needn't handle non-finite values.
Results may differ from a plain program's by a relative error of at most 0.015.
Values may be sent and summed in bfloat16 or wider, within the bound.
A program may use at most 128 MiB of HBM per device.

v0:
```python
import jax
import jax.numpy as jnp
from jax import lax
from jax.sharding import PartitionSpec as P

eps_norm = 1e-06


def on_device(
    attn_heads, o_weight, resid, norm_gain, expert_ids, combine_weights, w_gate_up, w_down
):
    tok_rows, width = resid.shape
    top_count = expert_ids.shape[1]
    num_experts = w_gate_up.shape[0] * lax.axis_size("expert")
    capacity = max(
        2, min(tok_rows, (4 * tok_rows * top_count + 3 * num_experts - 1) // (3 * num_experts))
    )
    partial = jnp.dot(attn_heads, o_weight, preferred_element_type=jnp.float32).astype(jnp.bfloat16)
    attn_out = lax.psum_scatter(partial, "tensor", scatter_dimension=0, tiled=True)
    gate_up_all = lax.all_gather(jnp.swapaxes(w_gate_up[0], 1, 2), "tensor", axis=0)
    down_all = lax.all_gather(w_down[0], "tensor", axis=0, tiled=True)
    mixed = resid.astype(jnp.float32) + attn_out.astype(jnp.float32)
    scale = lax.rsqrt(jnp.mean(mixed * mixed, axis=1, keepdims=True) + eps_norm)
    normed = (mixed * scale * norm_gain[None, :]).astype(jnp.bfloat16)
    named = expert_ids[:, :, None] == jnp.arange(num_experts, dtype=jnp.int32)[None, None, :]
    holds = jnp.any(named, axis=1)
    row = jnp.arange(tok_rows, dtype=jnp.int32)
    earlier = (row[None, :] < row[:, None]).astype(jnp.bfloat16)
    rank = jnp.dot(earlier, holds.astype(jnp.bfloat16), preferred_element_type=jnp.float32)
    rank = jnp.where(holds, rank.astype(jnp.int32), -1)
    weight = jnp.sum(jnp.where(named, combine_weights[:, :, None], 0.0), axis=1)
    slot = jnp.arange(capacity, dtype=jnp.int32)
    place = rank[:, :, None] == slot[None, None, :]
    pick = place.astype(jnp.bfloat16).reshape(tok_rows, num_experts * capacity)
    outgoing = lax.dot_general(
        pick, normed, (((0,), (0,)), ((), ())), preferred_element_type=jnp.float32
    ).astype(jnp.bfloat16)
    received = lax.all_to_all(
        outgoing.reshape(num_experts, capacity, width),
        "expert",
        split_axis=0,
        concat_axis=0,
        tiled=True,
    ).reshape(-1, width)
    total = jnp.zeros(received.shape, jnp.float32)
    gate = lax.dot_general(
        received,
        gate_up_all[:, 0].reshape(-1, width),
        (((1,), (1,)), ((), ())),
        preferred_element_type=jnp.float32,
    )
    up = lax.dot_general(
        received,
        gate_up_all[:, 1].reshape(-1, width),
        (((1,), (1,)), ((), ())),
        preferred_element_type=jnp.float32,
    )
    hidden = (jax.nn.silu(gate) * up).astype(jnp.bfloat16)
    total = jnp.dot(hidden, down_all, preferred_element_type=jnp.float32).astype(jnp.bfloat16)
    returned = lax.all_to_all(
        total.reshape(num_experts, capacity, width),
        "expert",
        split_axis=0,
        concat_axis=0,
        tiled=True,
    ).reshape(-1, width)
    spread = jnp.where(place, weight[:, :, None], 0.0).reshape(tok_rows, num_experts * capacity)
    high = spread.astype(jnp.bfloat16)
    low = (spread - high.astype(jnp.float32)).astype(jnp.bfloat16)
    moe_out = jnp.dot(high, returned, preferred_element_type=jnp.float32) + jnp.dot(
        low, returned, preferred_element_type=jnp.float32
    )
    return (mixed + moe_out).astype(jnp.bfloat16)


def solution(mesh):
    in_specs = (
        P("expert", "tensor"),
        P("tensor", None),
        P(("expert", "tensor"), None),
        P(),
        P(("expert", "tensor"), None),
        P(("expert", "tensor"), None),
        P("expert", None, None, "tensor"),
        P("expert", "tensor", None),
    )
    out_specs = P(("expert", "tensor"), None)
    return jax.shard_map(
        on_device, mesh=mesh, in_specs=in_specs, out_specs=out_specs, check_vma=False
    )
```

profile of v0, /device:TPU:8, one launch (start us, length us, event | category | flops | bytes accessed | tf_op | source)
XLA Modules:
  0.0 375.5 jit_solution(17430441759420197268)
XLA Ops:
  6.5 0.0 copy-start
  6.5 0.0 reduce-scatter.2.cloned.1.call-start
  6.5 1.6 copy-done
  8.1 3.7 convolution_convert_fusion.1
  11.8 0.0 copy-start.5
  11.8 0.0 copy-start.2
  11.8 0.0 reduce-scatter.2.cloned.1.call-update
  11.8 0.0 copy-start.4
  11.8 0.0 all-gather.5.cloned.1.call-start
  11.9 0.7 all-gather.5.cloned.1.call-update
  12.6 0.0 all-gather.7.cloned.1.call-start
  12.6 0.7 all-gather.7.cloned.1.call-update
  13.3 0.1 eq.48
  13.5 0.0 copy-done.5
  13.5 0.1 fusion.10
  13.7 33.3 %reduce-scatter.2.cloned.1.call-done = bf16[128,2048]{1,0:T(8,128)(2,1)} async-done(((bf16[512,2048]{1,0:T(8,128)(2,1)}), bf16[128,2048]{1,0:T(8,128)(2,1)}) %reduce-scatter.2.cloned.1.call-update) | async-done | bytes 524304 | tf_op jit(solution)/shard_map/reduce_scatter | solution.py:19
  47.1 0.0 copy-done.2
  47.1 1.3 multiply_reduce_fusion
  48.4 0.0 copy-done.4
  48.4 3.6 convolution_convert_fusion
  52.0 4.8 %reshape.42 = bf16[64,11,2048]{2,1,0:T(8,128)(2,1)} reshape(bf16[704,2048]{1,0:T(8,128)(2,1)} %convolution_convert_fusion) | data formatting | bytes 5767168 | tf_op jit(solution)/shard_map/reshape | solution.py:39
  56.8 106.9 %all_to_all.10 = bf16[64,11,2048]{2,1,0:T(8,128)(2,1)} all-to-all(bf16[64,11,2048]{2,1,0:T(8,128)(2,1)} %reshape.42), channel_id=1, replica_groups=mesh['expert'=64,'tensor'=4] {'expert'}, dimensions={0} | all-to-all | bytes 5767168 | tf_op jit(solution)/shard_map/all_to_all | solution.py:38
  163.6 4.8 %reshape.43 = bf16[704,2048]{1,0:T(8,128)(2,1)} reshape(bf16[64,11,2048]{2,1,0:T(8,128)(2,1)} %all_to_all.10) | data formatting | bytes 5767168 | tf_op jit(solution)/shard_map/reshape | solution.py:44
  168.5 0.0 all-gather.5.cloned.1.call-done
  168.5 11.6 %fusion.26 = (bf16[4,1,352,2048]{3,2,1,0:T(8,128)(2,1)}, bf16[4,1,352,2048]{3,2,1,0:T(8,128)(2,1)}) fusion(bf16[4,2,352,2048]{3,2,1,0:T(8,128)(2,1)} %bitcast.39), kind=kLoop, calls=%fused_computation.39 | loop fusion | bytes 23068672 | tf_op jit(solution)/shard_map/slice | solution.py:54
  180.1 10.1 %fusion.27 = f32[704,1408]{1,0:T(8,128)} fusion(bf16[704,2048]{1,0:T(8,128)(2,1)} %reshape.43, bf16[1408,2048]{1,0:T(8,128)(2,1)} %bitcast.41), kind=kOutput, calls=%fused_computation.40 | convolution fusion | flops 4060086272 | bytes 12615680 | tf_op jit(solution)/shard_map/dot_general | solution.py:46
  190.2 37.8 %all-gather.7.cloned.1.call-done = bf16[1,1408,2048]{2,1,0:T(8,128)(2,1)} async-done(((bf16[1,352,2048]{2,1,0:T(8,128)(2,1)}), bf16[1,1408,2048]{2,1,0:T(8,128)(2,1)}) %all-gather.7.cloned.1.call-update) | async-done | bytes 5767184 | tf_op jit(solution)/shard_map/all_gather | solution.py:21
  227.9 17.3 %fusion.2 = bf16[704,2048]{1,0:T(8,128)(2,1)} fusion(bf16[1,1408,2048]{2,1,0:T(8,128)(2,1)} %all-gather.7.cloned.1.call-done, f32[704,1408]{1,0:T(8,128)} %fusion.27, bf16[704,2048]{1,0:T(8,128)(2,1)} %reshape.43, bf16[1408,2048]{1,0:T(8,128)(2,1)} %bitcast.40), kind=kOutput, calls=%fused_computation.4 | convolution fusion | flops 8127561728 | bytes 21266432 | tf_op jit(solution)/shard_map/dot_general | solution.py:59
  245.3 4.8 %reshape.44 = bf16[64,11,2048]{2,1,0:T(8,128)(2,1)} reshape(bf16[704,2048]{1,0:T(8,128)(2,1)} %fusion.2) | data formatting | bytes 5767168 | tf_op jit(solution)/shard_map/reshape | solution.py:61
  250.0 0.0 copy-start.6
  250.0 10.9 %all-to-all-start.1 = ((bf16[64,11,2048]{2,1,0:T(8,128)(2,1)}), bf16[64,11,2048]{2,1,0:T(8,128)(2,1)}, u32[]{:S(2)}, u32[]{:S(2)}) async-start(bf16[64,11,2048]{2,1,0:T(8,128)(2,1)} %reshape.44), calls=%async_computation.2 | async-start | bytes 8388608 | tf_op jit(solution)/shard_map/all_to_all | solution.py:60
  260.9 0.0 copy-done.6
  260.9 0.0 copy-start.3
  260.9 0.0 copy-start.1
  261.0 96.1 %all-to-all-done.1 = bf16[64,11,2048]{2,1,0:T(8,128)(2,1)} async-done(((bf16[64,11,2048]{2,1,0:T(8,128)(2,1)}), bf16[64,11,2048]{2,1,0:T(8,128)(2,1)}, u32[]{:S(2)}, u32[]{:S(2)}) %all-to-all-start.1) | async-done | bytes 2883616 | tf_op jit(solution)/shard_map/all_to_all | solution.py:60
  357.0 5.5 %convolution_bitcast_fusion = f32[128,2048]{1,0:T(8,128)S(1)} fusion(bf16[64,11,2048]{2,1,0:T(8,128)(2,1)} %all-to-all-done.1, f32[128,64]{0,1:T(8,128)S(1)} %select_reduce_fusion, s32[128,64]{0,1:T(8,128)S(1)} %fusion.10), kind=kOutput, calls=%fused_computation.6 | convolution fusion | flops 369639424 | bytes 3997696 | tf_op jit(solution)/shard_map/dot_general | solution.py:70
  362.6 0.0 copy-done.3
  362.6 6.4 %fusion.7 = bf16[128,2048]{1,0:T(8,128)(2,1)} fusion(f32[128,2048]{1,0:T(8,128)S(1)} %convolution_bitcast_fusion, bf16[64,11,2048]{2,1,0:T(8,128)(2,1)} %all-to-all-done.1, bf16[128,2048]{1,0:T(8,128)(2,1)S(1)} %copy-done.3, bf16[128,2048]{1,0:T(8,128)(2,1)S(1)} %copy-done.2, f32[128,64]{0,1:T(8,128)S(1)} %select_reduce_fusion, s32[128,64]{0,1:T(8,128)S(1)} %fusion.10), kind=kOutput, calls=%fused_computation.10 | convolution fusion | flops 370851840 | bytes 5570560 | tf_op jit(solution)/shard_map/dot_general | solution.py:70
  369.0 0.0 copy-done.1
  (6 shorter events, 0.1 us)
Async XLA Ops:
  6.5 1.6 copy-start
  6.5 40.5 %reduce-scatter.2.cloned.1.call-start = ((), (), s32[]{:S(2)}) async-start(), calls=%async_computation.3 | async-start | bytes 2621440 | tf_op jit(solution)/shard_map/reduce_scatter | solution.py:19
  11.8 1.7 copy-start.5
  11.8 35.3 %copy-start.2 = (bf16[128,2048]{1,0:T(8,128)(2,1)S(1)}, bf16[128,2048]{1,0:T(8,128)(2,1)}, u32[]{:S(2)}) copy-start(bf16[128,2048]{1,0:T(8,128)(2,1)} %param.10) | copy-start | bytes 1572868
  11.8 36.6 %copy-start.4 = (f32[2048]{0:T(1024)S(1)}, f32[2048]{0:T(1024)}, u32[]{:S(2)}) copy-start(f32[2048]{0:T(1024)} %param.11) | copy-start | bytes 24580
  11.8 156.6 %all-gather.5.cloned.1.call-start = ((), (), s32[]{:S(2)}) async-start(), calls=%async_computation.4 | async-start | bytes 14417920 | tf_op jit(solution)/shard_map/all_gather | solution.py:20
  12.6 215.4 %all-gather.7.cloned.1.call-start = ((), (), s32[]{:S(2)}) async-start(), calls=%async_computation.5 | async-start | bytes 7208960 | tf_op jit(solution)/shard_map/all_gather | solution.py:21
  250.0 10.9 %copy-start.6 = (f32[128,4]{0,1:T(4,128)S(1)}, f32[128,4]{0,1:T(4,128)}, u32[]{:S(2)}) copy-start(f32[128,4]{0,1:T(4,128)} %param.13) | copy-start | bytes 6148
  250.0 107.0 %all-to-all-start.1 = ((bf16[64,11,2048]{2,1,0:T(8,128)(2,1)}), bf16[64,11,2048]{2,1,0:T(8,128)(2,1)}, u32[]{:S(2)}, u32[]{:S(2)}) async-start(bf16[64,11,2048]{2,1,0:T(8,128)(2,1)} %reshape.44), calls=%async_computation.2 | async-start | bytes 8388608 | tf_op jit(solution)/shard_map/all_to_all | solution.py:60
  260.9 101.7 %copy-start.3 = (bf16[128,2048]{1,0:T(8,128)(2,1)S(1)}, bf16[128,2048]{1,0:T(8,128)(2,1)}, u32[]{:S(2)}) copy-start(bf16[128,2048]{1,0:T(8,128)(2,1)} %reduce-scatter.2.cloned.1.call-done) | copy-start | bytes 1572868
  260.9 108.1 %copy-start.1 = (bf16[512,2048]{1,0:T(8,128)(2,1)S(1)}, bf16[512,2048]{1,0:T(8,128)(2,1)}, u32[]{:S(2)}) copy-start(bf16[512,2048]{1,0:T(8,128)(2,1)} %param.9) | copy-start | bytes 6291460
Sparse Core Ops, SparseCore 0:
  11.9 35.0 reduce-scatter.1
  49.0 112.0 all-gather.4
  163.0 64.8 all-gather.6
where the time goes:
time: 376 us
  waiting for transfers between devices  169 us (45%)
  blocking collectives  107 us (28%)
  matrix products  46.8 us (12%)
  local copies, waits for them, and re-layouts  27.8 us (7%)
  between operations  13.2 us (4%)
  starting transfers between devices  11 us (3%)
    all_to_all x1, blocking collectives, on_device(): lax.all_to_all(outgoing.reshape(num_experts, capacity, width), 'expert',...  107 us
    all_to_all x1, waiting for transfers between devices, on_device(): lax.all_to_all(total.reshape(num_experts, capacity, width), 'expert', spl...  96.1 us
    all_gather x1, waiting for transfers between devices, on_device(): down_all = lax.all_gather(w_down[0], 'tensor', axis=0, tiled=True)  37.8 us
    reduce_scatter x1, waiting for transfers between devices, on_device(): lax.psum_scatter(partial, 'tensor', scatter_dimension=0, tiled=True)  33.3 us
    dot_general x1, matrix products, on_device(): jnp.dot(hidden, down_all, preferred_element_type=jnp.float32)  17.3 us
    slice x1, local copies, waits for them, and re-layouts, on_device(): gate_up_all[:, 1].reshape(-1, width)  11.6 us
    all_to_all x1, starting transfers between devices, on_device(): lax.all_to_all(total.reshape(num_experts, capacity, width), 'expert', spl...  10.9 us
    dot_general x1, matrix products, on_device(): lax.dot_general(received, gate_up_all[:, 0].reshape(-1, width), (((1,), (...  10.1 us
  transfers between devices with their start and end apart: 4, of which 3 were waited for; matrix products, arithmetic and copies ran while one was open for 10% of the time, Pallas kernels for 0%

commit v1 on v0

--- a/solution.py
+++ b/solution.py
@@ -18,7 +18,9 @@
     partial = jnp.dot(attn_heads, o_weight, preferred_element_type=jnp.float32).astype(jnp.bfloat16)
     attn_out = lax.psum_scatter(partial, "tensor", scatter_dimension=0, tiled=True)
     gate_up_all = lax.all_gather(jnp.swapaxes(w_gate_up[0], 1, 2), "tensor", axis=0)
-    down_all = lax.all_gather(w_down[0], "tensor", axis=0, tiled=True)
+    down_all = jnp.concatenate(
+        lax.all_to_all(jnp.stack([w_down[0]] * lax.axis_size("tensor")), "tensor", 0, 0), axis=0
+    )
     mixed = resid.astype(jnp.float32) + attn_out.astype(jnp.float32)
     scale = lax.rsqrt(jnp.mean(mixed * mixed, axis=1, keepdims=True) + eps_norm)
     normed = (mixed * scale * norm_gain[None, :]).astype(jnp.bfloat16)

time: 376 us -> 382 us (1.016)
    all_to_all x0 -> x1, waiting for transfers between devices: none -> 38.7 us  [on_device(): lax.all_to_all(jnp.stack([w_down[0]] * lax.axis_size('tensor')), 'tensor'...]
    all_gather x1 -> x0, waiting for transfers between devices: 37.8 us -> none  [on_device(): down_all = lax.all_gather(w_down[0], 'tensor', axis=0, tiled=True)]
    all_to_all x0 -> x1, starting transfers between devices: none -> 5.17 us  [on_device(): lax.all_to_all(jnp.stack([w_down[0]] * lax.axis_size('tensor')), 'tensor'...]
where the time goes in v1:
time: 382 us; the launch traced here: 381 us
  waiting for transfers between devices  170 us (45%)
  blocking collectives  107 us (28%)
  matrix products  46.7 us (12%)
  local copies, waits for them, and re-layouts  30.5 us (8%)
  between operations  13.5 us (4%)
  starting transfers between devices  12.4 us (3%)
    all_to_all x1, blocking collectives, on_device(): lax.all_to_all(outgoing.reshape(num_experts, capacity, width), 'expert',...  107 us
    all_to_all x1, waiting for transfers between devices, on_device(): lax.all_to_all(total.reshape(num_experts, capacity, width), 'expert', spl...  96.1 us
    all_to_all x1, waiting for transfers between devices, on_device(): lax.all_to_all(jnp.stack([w_down[0]] * lax.axis_size('tensor')), 'tensor'...  38.7 us
    reduce_scatter x1, waiting for transfers between devices, on_device(): lax.psum_scatter(partial, 'tensor', scatter_dimension=0, tiled=True)  34.1 us
    dot_general x1, matrix products, on_device(): jnp.dot(hidden, down_all, preferred_element_type=jnp.float32)  17.3 us
    slice x1, local copies, waits for them, and re-layouts, on_device(): gate_up_all[:, 1].reshape(-1, width)  11 us
    dot_general x1, matrix products, on_device(): lax.dot_general(received, gate_up_all[:, 0].reshape(-1, width), (((1,), (...  10 us
  transfers between devices with their start and end apart: 4, of which 3 were waited for; matrix products, arithmetic and copies ran while one was open for 10% of the time, Pallas kernels for 0%

profile of v1, /device:TPU:8, one launch (start us, length us, event | category | flops | bytes accessed | tf_op | source)
XLA Modules:
  0.0 381.0 jit_solution(6226123497719292427)
XLA Ops:
  6.5 0.0 copy-start
  6.5 0.0 reduce-scatter.2.cloned.1.call-start
  6.5 1.6 copy-done
  8.1 3.7 convolution_convert_fusion.2
  11.8 0.0 copy-start.6
  11.8 0.0 copy-start.2
  11.8 0.0 copy-start.5
  11.9 0.0 reduce-scatter.2.cloned.1.call-update
  11.9 0.0 all-gather.3.cloned.1.call-start
  11.9 0.7 all-gather.3.cloned.1.call-update
  12.6 0.1 eq.48
  12.8 0.0 copy-done.6
  12.8 0.1 fusion.5
  13.1 34.1 %reduce-scatter.2.cloned.1.call-done = bf16[128,2048]{1,0:T(8,128)(2,1)} async-done(((bf16[512,2048]{1,0:T(8,128)(2,1)}), bf16[128,2048]{1,0:T(8,128)(2,1)}) %reduce-scatter.2.cloned.1.call-update) | async-done | bytes 524304 | tf_op jit(solution)/shard_map/reduce_scatter | solution.py:19
  47.1 0.0 copy-done.2
  47.1 1.3 multiply_reduce_fusion
  48.4 0.0 copy-done.5
  48.4 3.6 convolution_convert_fusion
  52.0 4.8 %reshape.46 = bf16[64,11,2048]{2,1,0:T(8,128)(2,1)} reshape(bf16[704,2048]{1,0:T(8,128)(2,1)} %convolution_convert_fusion) | data formatting | bytes 5767168 | tf_op jit(solution)/shard_map/reshape | solution.py:41
  56.8 0.0 copy-start.4
  56.8 107.0 %all_to_all.15 = bf16[64,11,2048]{2,1,0:T(8,128)(2,1)} all-to-all(bf16[64,11,2048]{2,1,0:T(8,128)(2,1)} %reshape.46), channel_id=1, replica_groups=mesh['expert'=64,'tensor'=4] {'expert'}, dimensions={0} | all-to-all | bytes 5767168 | tf_op jit(solution)/shard_map/all_to_all | solution.py:40
  163.8 0.0 copy-done.4
  163.8 3.2 stack.3
  167.1 5.2 %all-to-all-start.1 = ((bf16[4,352,2048]{2,1,0:T(8,128)(2,1)}), bf16[4,352,2048]{2,1,0:T(8,128)(2,1)}, u32[]{:S(2)}, u32[]{:S(2)}) async-start(bf16[4,352,2048]{2,1,0:T(8,128)(2,1)} %stack.3), calls=%async_computation.2 | async-start | bytes 11534336 | tf_op jit(solution)/shard_map/all_to_all | solution.py:22
  172.2 4.9 %reshape.47 = bf16[704,2048]{1,0:T(8,128)(2,1)} reshape(bf16[64,11,2048]{2,1,0:T(8,128)(2,1)} %all_to_all.15) | data formatting | bytes 5767168 | tf_op jit(solution)/shard_map/reshape | solution.py:46
  177.1 0.0 all-gather.3.cloned.1.call-done
  177.1 11.0 %fusion.22 = (bf16[4,1,352,2048]{3,2,1,0:T(8,128)(2,1)}, bf16[4,1,352,2048]{3,2,1,0:T(8,128)(2,1)}) fusion(bf16[4,2,352,2048]{3,2,1,0:T(8,128)(2,1)} %bitcast.28), kind=kLoop, calls=%fused_computation.38 | loop fusion | bytes 23068672 | tf_op jit(solution)/shard_map/slice | solution.py:56
  188.1 10.0 %fusion.23 = f32[704,1408]{1,0:T(8,128)} fusion(bf16[704,2048]{1,0:T(8,128)(2,1)} %reshape.47, bf16[1408,2048]{1,0:T(8,128)(2,1)} %bitcast.30), kind=kOutput, calls=%fused_computation.39 | convolution fusion | flops 4060086272 | bytes 12615680 | tf_op jit(solution)/shard_map/dot_general | solution.py:48
  198.1 38.7 %all-to-all-done.1 = bf16[4,352,2048]{2,1,0:T(8,128)(2,1)} async-done(((bf16[4,352,2048]{2,1,0:T(8,128)(2,1)}), bf16[4,352,2048]{2,1,0:T(8,128)(2,1)}, u32[]{:S(2)}, u32[]{:S(2)}) %all-to-all-start.1) | async-done | bytes 5767200 | tf_op jit(solution)/shard_map/all_to_all | solution.py:22
  236.8 17.3 %convolution_convert_fusion.1 = bf16[704,2048]{1,0:T(8,128)(2,1)} fusion(bf16[1408,2048]{1,0:T(8,128)(2,1)} %bitcast.6, f32[704,1408]{1,0:T(8,128)} %fusion.23, bf16[704,2048]{1,0:T(8,128)(2,1)} %reshape.47, bf16[1408,2048]{1,0:T(8,128)(2,1)} %bitcast.29), kind=kOutput, calls=%fused_computation.2 | convolution fusion | flops 8127561728 | bytes 21266432 | tf_op jit(solution)/shard_map/dot_general | solution.py:61
  254.1 4.8 %reshape.49 = bf16[64,11,2048]{2,1,0:T(8,128)(2,1)} reshape(bf16[704,2048]{1,0:T(8,128)(2,1)} %convolution_convert_fusion.1) | data formatting | bytes 5767168 | tf_op jit(solution)/shard_map/reshape | solution.py:63
  258.9 0.0 copy-start.7
  258.9 7.2 %all-to-all-start.2 = ((bf16[64,11,2048]{2,1,0:T(8,128)(2,1)}), bf16[64,11,2048]{2,1,0:T(8,128)(2,1)}, u32[]{:S(2)}, u32[]{:S(2)}) async-start(bf16[64,11,2048]{2,1,0:T(8,128)(2,1)} %reshape.49), calls=%async_computation.3 | async-start | bytes 8388608 | tf_op jit(solution)/shard_map/all_to_all | solution.py:62
  266.1 0.0 copy-done.7
  266.1 0.0 copy-start.3
  266.1 0.0 copy-start.1
  266.1 96.1 %all-to-all-done.2 = bf16[64,11,2048]{2,1,0:T(8,128)(2,1)} async-done(((bf16[64,11,2048]{2,1,0:T(8,128)(2,1)}), bf16[64,11,2048]{2,1,0:T(8,128)(2,1)}, u32[]{:S(2)}, u32[]{:S(2)}) %all-to-all-start.2) | async-done | bytes 2883616 | tf_op jit(solution)/shard_map/all_to_all | solution.py:62
  362.2 5.5 %convolution_bitcast_fusion = f32[128,2048]{1,0:T(8,128)S(1)} fusion(bf16[64,11,2048]{2,1,0:T(8,128)(2,1)} %all-to-all-done.2, f32[128,64]{0,1:T(8,128)S(1)} %select_reduce_fusion, s32[128,64]{0,1:T(8,128)S(1)} %fusion.5), kind=kOutput, calls=%fused_computation.4 | convolution fusion | flops 369639424 | bytes 3997696 | tf_op jit(solution)/shard_map/dot_general | solution.py:72
  367.7 0.0 copy-done.3
  367.7 6.4 %fusion.2 = bf16[128,2048]{1,0:T(8,128)(2,1)} fusion(f32[128,2048]{1,0:T(8,128)S(1)} %convolution_bitcast_fusion, bf16[64,11,2048]{2,1,0:T(8,128)(2,1)} %all-to-all-done.2, bf16[128,2048]{1,0:T(8,128)(2,1)S(1)} %copy-done.3, bf16[128,2048]{1,0:T(8,128)(2,1)S(1)} %copy-done.2, f32[128,64]{0,1:T(8,128)S(1)} %select_reduce_fusion, s32[128,64]{0,1:T(8,128)S(1)} %fusion.5), kind=kOutput, calls=%fused_computation.8 | convolution fusion | flops 370851840 | bytes 5570560 | tf_op jit(solution)/shard_map/dot_general | solution.py:72
  374.1 0.0 copy-done.1
  (6 shorter events, 0.1 us)
Async XLA Ops:
  6.5 1.6 copy-start
  6.5 40.6 %reduce-scatter.2.cloned.1.call-start = ((), (), s32[]{:S(2)}) async-start(), calls=%async_computation.4 | async-start | bytes 2621440 | tf_op jit(solution)/shard_map/reduce_scatter | solution.py:19
  11.8 0.9 copy-start.6
  11.8 35.3 %copy-start.2 = (bf16[128,2048]{1,0:T(8,128)(2,1)S(1)}, bf16[128,2048]{1,0:T(8,128)(2,1)}, u32[]{:S(2)}) copy-start(bf16[128,2048]{1,0:T(8,128)(2,1)} %param.10) | copy-start | bytes 1572868
  11.8 36.6 %copy-start.5 = (f32[2048]{0:T(1024)S(1)}, f32[2048]{0:T(1024)}, u32[]{:S(2)}) copy-start(f32[2048]{0:T(1024)} %param.11) | copy-start | bytes 24580
  11.9 165.2 %all-gather.3.cloned.1.call-start = ((), (), s32[]{:S(2)}) async-start(), calls=%async_computation.5 | async-start | bytes 14417920 | tf_op jit(solution)/shard_map/all_gather | solution.py:20
  56.8 107.0 %copy-start.4 = (bf16[1,352,2048]{2,1,0:T(8,128)(2,1)S(1)}, bf16[1,352,2048]{2,1,0:T(8,128)(2,1)}, u32[]{:S(2)}) copy-start(bf16[1,352,2048]{2,1,0:T(8,128)(2,1)} %param.15) | copy-start | bytes 4325380
  167.1 69.8 %all-to-all-start.1 = ((bf16[4,352,2048]{2,1,0:T(8,128)(2,1)}), bf16[4,352,2048]{2,1,0:T(8,128)(2,1)}, u32[]{:S(2)}, u32[]{:S(2)}) async-start(bf16[4,352,2048]{2,1,0:T(8,128)(2,1)} %stack.3), calls=%async_computation.2 | async-start | bytes 11534336 | tf_op jit(solution)/shard_map/all_to_all | solution.py:22
  258.9 7.2 %copy-start.7 = (f32[128,4]{0,1:T(4,128)S(1)}, f32[128,4]{0,1:T(4,128)}, u32[]{:S(2)}) copy-start(f32[128,4]{0,1:T(4,128)} %param.13) | copy-start | bytes 6148
  258.9 103.3 %all-to-all-start.2 = ((bf16[64,11,2048]{2,1,0:T(8,128)(2,1)}), bf16[64,11,2048]{2,1,0:T(8,128)(2,1)}, u32[]{:S(2)}, u32[]{:S(2)}) async-start(bf16[64,11,2048]{2,1,0:T(8,128)(2,1)} %reshape.49), calls=%async_computation.3 | async-start | bytes 8388608 | tf_op jit(solution)/shard_map/all_to_all | solution.py:62
  266.1 101.7 %copy-start.3 = (bf16[128,2048]{1,0:T(8,128)(2,1)S(1)}, bf16[128,2048]{1,0:T(8,128)(2,1)}, u32[]{:S(2)}) copy-start(bf16[128,2048]{1,0:T(8,128)(2,1)} %reduce-scatter.2.cloned.1.call-done) | copy-start | bytes 1572868
  266.1 108.1 %copy-start.1 = (bf16[512,2048]{1,0:T(8,128)(2,1)S(1)}, bf16[512,2048]{1,0:T(8,128)(2,1)}, u32[]{:S(2)}) copy-start(bf16[512,2048]{1,0:T(8,128)(2,1)} %param.9) | copy-start | bytes 6291460
Sparse Core Ops, SparseCore 0:
  12.0 35.0 reduce-scatter.1
  49.1 112.0 all-gather.2
